TPU v7x, 128 devices: a whole 4x4x4 slice. The times are simulated.
128 devices in a mesh: dev: 128 (over y, x, z, core).
Axes of the slice: x: 4, y: 4, z: 4, core: 2. Of those that a mesh axis runs over, the one named last changes fastest.
Arguments:
- queries: bfloat16 [256, 32, 128], P('dev'), may hold values from -0.119628906 to 0.119628906
- passages: bfloat16 [65536, 64, 128], P('dev'), may hold values from -1.796875 to 1.796875
- lengths: int32 [65536], P('dev'), may hold values from 16 to 64
- candidates: int32 [256, 64], P('dev'), may hold values from 0 to 65535, as said below
Outputs:
- scores: float32 [256, 64], P('dev')
Inputs may be any that keep to these rules, and one draw needn't show every extreme that they name: `candidates`: the 128 entries of the rows held by one device name, with repetition, at most 2 passages held by any one device (passage p is held by device p // 512), and exactly 2 for four devices; the passages of low number within each device are named far more often than the others, and a few devices are named far more often than the others over all rows.
All inputs are finite; a program needn't handle non-finite values.
Results may differ from a plain program's by a relative error of at most 0.0003.
Values may be sent and summed in bfloat16 or wider, within the bound.
A program may use at most 64 MiB of HBM per device.

v0:
```python
import jax
import jax.numpy as jnp
from jax import lax
from jax.sharding import PartitionSpec as P


def masked_maxsim(similarity_matrix, live):
    keep = jnp.arange(similarity_matrix.shape[-1])[None, None, :] < live[:, None, None]
    return jnp.sum(jnp.max(jnp.where(keep, similarity_matrix, -1e30), axis=2), axis=1)


def on_device(queries, passages, lengths, candidates):
    count = lax.axis_size("dev")
    q_local, qtok, dim = queries.shape
    p_local, ptok = (passages.shape[0], passages.shape[1])
    cand = candidates.shape[1]
    slots = q_local * cand
    cap = 2 * ((slots + count - 1) // count)
    flat = candidates.reshape(-1)
    owner = flat // p_local
    local = flat % p_local
    query_of = jnp.arange(slots, dtype=jnp.int32) // cand
    indicator_matrix = (owner[:, None] == jnp.arange(count, dtype=jnp.int32)[None, :]).astype(
        jnp.int32
    )
    rank = jnp.sum(
        (jnp.cumsum(indicator_matrix, axis=0) - indicator_matrix) * indicator_matrix, axis=1
    )
    slot = owner * cap + rank
    code = query_of * p_local + local
    request_ids = jnp.zeros((count * cap,), jnp.int32).at[slot].set(code).reshape(count, cap)
    arrived = lax.all_to_all(request_ids, "dev", split_axis=0, concat_axis=0, tiled=True)
    wanted = arrived % p_local
    block_groups = passages[wanted.reshape(-1)].reshape(count, cap, ptok, dim)
    block_length_total = lengths[wanted].astype(jnp.bfloat16)
    back, back_len = (
        lax.all_to_all(block_groups, "dev", split_axis=0, concat_axis=0, tiled=True),
        lax.all_to_all(block_length_total, "dev", split_axis=0, concat_axis=0, tiled=True),
    )
    owned_passages = back.reshape(count * cap, ptok, dim)[slot].reshape(q_local, cand, ptok, dim)
    mine_len = back_len.reshape(-1)[slot].astype(jnp.int32)
    similarity_matrix = jnp.einsum(
        "wyf,wrjf->wryj", queries, owned_passages, preferred_element_type=jnp.float32
    )
    similarity_matrix = similarity_matrix.reshape(slots, qtok, ptok)
    final_scores = masked_maxsim(similarity_matrix, mine_len)
    return final_scores.reshape(q_local, cand)


def solution(mesh):
    return jax.shard_map(
        on_device,
        mesh=mesh,
        in_specs=(P("dev", None, None), P("dev", None, None), P("dev"), P("dev", None)),
        out_specs=P("dev", None),
        check_vma=False,
    )
```

profile of v0, /device:TPU:1, one launch (start us, length us, event | category | flops | bytes accessed | tf_op | source)
XLA Modules:
  0.0 108.2 jit_solution(4828823981467604372)
XLA Ops:
  0.0 0.8 reshape.290
  0.8 0.8 reshape.289
  1.7 0.2 reduce_window_sum.11
  1.8 0.2 select_reduce_fusion.1
  2.0 1.0 scatter_custom_fusion
  3.0 0.1 all_to_all.17
  3.1 20.7 %all_to_all.26 = s32[128,1,2]{2,1,0:T(1,128)S(1)} all-to-all(s32[128,1,2]{2,1,0:T(1,128)S(1)} %bitcast.24), channel_id=1, replica_groups=mesh['dev'=128] {'dev'}, dimensions={0} | all-to-all | bytes 2048 | tf_op jit(solution)/shard_map/all_to_all | solution.py:32
  23.9 0.5 broadcast.284
  24.4 0.8 reduce.7
  25.2 0.1 all_to_all.21
  25.4 0.1 reshape.298
  25.5 1.9 %gather_fusion = s32[256]{0:T(256)S(1)} fusion(s32[512]{0:T(512)S(1)} %copy-done.1, s32[1024]{0:T(1024)S(1)} %pad_clamp_fusion.2), kind=kCustom, calls=%fused_computation | custom fusion | bytes 3072 | tf_op jit(solution)/shard_map/gather | solution.py:35
  27.5 0.8 convert_element_type.34
  28.3 4.6 %all-to-all-start.1 = ((bf16[128,1,2]{2,1,0:T(2,128)(2,1)}), bf16[128,1,2]{2,1,0:T(2,128)(2,1)S(1)}, u32[]{:S(2)}, u32[]{:S(2)}) async-start(bf16[128,1,2]{2,1,0:T(2,128)(2,1)} %convert_element_type.34), calls=%async_computation.1 | async-start | bytes 131072 | tf_op jit(solution)/shard_map/all_to_all | solution.py:38
  32.9 6.4 %gather_fusion.2 = bf16[256,64,128]{2,1,0:T(8,128)(2,1)} fusion(bf16[512,64,128]{2,1,0:T(8,128)(2,1)} %param.5, s32[1024]{0:T(1024)S(1)} %pad_clamp_fusion), kind=kCustom, calls=%fused_computation.2 | custom fusion | bytes 8389632 | tf_op jit(solution)/shard_map/gather | solution.py:34
  39.3 3.0 %all-to-all-done.1 = bf16[128,1,2]{2,1,0:T(2,128)(2,1)S(1)} async-done(((bf16[128,1,2]{2,1,0:T(2,128)(2,1)}), bf16[128,1,2]{2,1,0:T(2,128)(2,1)S(1)}, u32[]{:S(2)}, u32[]{:S(2)}) %all-to-all-start.1) | async-done | bytes 544 | tf_op jit(solution)/shard_map/all_to_all | solution.py:38
  42.4 7.2 %all-to-all-start.2 = ((bf16[128,2,64,128]{3,2,1,0:T(8,128)(2,1)}), bf16[128,2,64,128]{3,2,1,0:T(8,128)(2,1)}, u32[]{:S(2)}, u32[]{:S(2)}) async-start(bf16[128,2,64,128]{3,2,1,0:T(8,128)(2,1)} %bitcast.21), calls=%async_computation.2 | async-start | bytes 8388608 | tf_op jit(solution)/shard_map/all_to_all | solution.py:37
  49.6 0.2 reduce.3
  49.8 0.1 reshape.291
  50.0 1.2 %gather_fusion.1 = bf16[128]{0:T(256)(128)(2,1)S(1)} fusion(bf16[256]{0:T(256)(128)(2,1)S(1)} %reshape.291, s32[1024]{0:T(1024)S(1)} %pad_clamp_fusion.1), kind=kCustom, calls=%fused_computation.1 | custom fusion | bytes 1024 | tf_op jit(solution)/shard_map/gather | solution.py:41
  51.4 50.8 %all-to-all-done.2 = bf16[128,2,64,128]{3,2,1,0:T(8,128)(2,1)} async-done(((bf16[128,2,64,128]{3,2,1,0:T(8,128)(2,1)}), bf16[128,2,64,128]{3,2,1,0:T(8,128)(2,1)}, u32[]{:S(2)}, u32[]{:S(2)}) %all-to-all-start.2) | async-done | bytes 4194336 | tf_op jit(solution)/shard_map/all_to_all | solution.py:37
  102.2 3.1 %gather_fusion.3 = bf16[128,64,128]{2,1,0:T(8,128)(2,1)S(1)} fusion(bf16[256,64,128]{2,1,0:T(8,128)(2,1)} %bitcast.6, s32[1024]{0:T(1024)S(1)} %pad_clamp_fusion.1), kind=kCustom, calls=%fused_computation.3 | custom fusion | bytes 4194816 | tf_op jit(solution)/shard_map/gather | solution.py:40
  105.4 2.2 %select_reduce_fusion = f32[2,64,32]{2,1,0:T(8,128)S(1)} fusion(bf16[2,64,64,128]{3,2,1,0:T(8,128)(2,1)S(1)} %bitcast.22, pred[2,64,64]{2,1,0:T(8,128)(4,1)S(1)} %iota_compare_fusion.1, bf16[2,32,128]{2,1,0:T(8,128)(2,1)S(1)} %copy-done), kind=kOutput, calls=%fused_computation.5 | convolution fusion | flops 67629056 | bytes 2138112 | tf_op jit(solution)/shard_map/wyf,wrjf->wryj/dot_general | solution.py:42
  107.6 0.7 reduce_sum.22
  (16 shorter events, 0.4 us)
Async XLA Ops:
  0.0 105.4 %copy-start = (bf16[2,32,128]{2,1,0:T(8,128)(2,1)S(1)}, bf16[2,32,128]{2,1,0:T(8,128)(2,1)}, u32[]{:S(2)}) copy-start(bf16[2,32,128]{2,1,0:T(8,128)(2,1)} %param.4) | copy-start | bytes 49156
  0.0 25.5 %copy-start.1 = (s32[512]{0:T(512)S(1)}, s32[512]{0:T(512)}, u32[]{:S(2)}) copy-start(s32[512]{0:T(512)} %param.6) | copy-start | bytes 6148
  28.3 14.1 %all-to-all-start.1 = ((bf16[128,1,2]{2,1,0:T(2,128)(2,1)}), bf16[128,1,2]{2,1,0:T(2,128)(2,1)S(1)}, u32[]{:S(2)}, u32[]{:S(2)}) async-start(bf16[128,1,2]{2,1,0:T(2,128)(2,1)} %convert_element_type.34), calls=%async_computation.1 | async-start | bytes 131072 | tf_op jit(solution)/shard_map/all_to_all | solution.py:38
  42.4 59.8 %all-to-all-start.2 = ((bf16[128,2,64,128]{3,2,1,0:T(8,128)(2,1)}), bf16[128,2,64,128]{3,2,1,0:T(8,128)(2,1)}, u32[]{:S(2)}, u32[]{:S(2)}) async-start(bf16[128,2,64,128]{3,2,1,0:T(8,128)(2,1)} %bitcast.21), calls=%async_computation.2 | async-start | bytes 8388608 | tf_op jit(solution)/shard_map/all_to_all | solution.py:37
where the time goes:
time: 109 us; the launch traced here: 108 us
  waiting for transfers between devices  53.9 us (49%)
  blocking collectives  20.7 us (19%)
  local copies, waits for them, and re-layouts  17.2 us (16%)
  starting transfers between devices  11.8 us (11%)
  other arithmetic  2.27 us (2%)
  matrix products  2.16 us (2%)
    all_to_all x1, waiting for transfers between devices, on_device(): lax.all_to_all(block_groups, 'dev', split_axis=0, concat_axis=0, tiled=True)  50.8 us
    all_to_all x1, blocking collectives, on_device(): lax.all_to_all(request_ids, 'dev', split_axis=0, concat_axis=0, tiled=True)  20.7 us
    all_to_all x1, starting transfers between devices, on_device(): lax.all_to_all(block_groups, 'dev', split_axis=0, concat_axis=0, tiled=True)  7.23 us
    gather x1, local copies, waits for them, and re-layouts, on_device(): block_groups = passages[wanted.reshape(-1)].reshape(count, cap, ptok, dim)  6.4 us
    all_to_all x1, starting transfers between devices, on_device(): lax.all_to_all(block_length_total, 'dev', split_axis=0, concat_axis=0, ti...  4.6 us
    gather x1, local copies, waits for them, and re-layouts, on_device(): back.reshape(count * cap, ptok, dim)[slot].reshape(q_local, cand, ptok, dim)  3.14 us
    all_to_all x1, waiting for transfers between devices, on_device(): lax.all_to_all(block_length_total, 'dev', split_axis=0, concat_axis=0, ti...  3.03 us
  transfers between devices with their start and end apart: 2, of which 2 were waited for; matrix products, arithmetic and copies ran while one was open for 8% of the time, Pallas kernels for 0%

commit v1 on v0

v1 whole, which is shorter than its diff:
```python
import functools

import jax
import jax.numpy as jnp
from jax import lax
from jax.experimental import pallas as pl
from jax.experimental.pallas import tpu as pltpu
from jax.sharding import PartitionSpec as P

MESH = pl.DeviceIdType.MESH
N_DEV = 128
STRIDE = {"z": 2, "x": 8, "y": 32}
PARTS = ((0, 32, "zyx"), (32, 16, "xzy"), (48, 16, "yxz"))


def shifted(me, axis, k):
    stride = STRIDE[axis]
    digit = (me // stride) % 4
    return me + stride * ((digit + k) % 4 - digit)


def place(order, dev):
    at = dev % 2
    for axis in reversed(order):
        at = at * 4 + (dev // STRIDE[axis]) % 4
    return at


def kernel(
    q_ref, pas_hbm, len_ref, cand_ref, out_ref,
    ga, gb, gc, codes, pas, codes_s, best, send, recv,
    q_send, q_recv, sib_send, sib_recv, c_send, c_recv, pas_sem, smem_sem, r_send, r_recv,
):
    me = lax.axis_index("dev")
    core = me % 2
    sibling = me + 1 - 2 * core
    bufs = (ga, gb, gc)

    pas_copy = pltpu.make_async_copy(pas_hbm, pas, pas_sem)
    pas_copy.start()

    barrier = pltpu.get_barrier_semaphore()
    near = [sibling]
    for axis in "zxy":
        for k in (1, 2, 3):
            near.append(shifted(me, axis, k))
    for k in (1, 2, 3):
        near.append(shifted(sibling, "z", k))
    for d in near:
        pl.semaphore_signal(barrier, inc=1, device_id=(d,), device_id_type=MESH)

    cand = cand_ref[...]
    row = jnp.concatenate([cand[0:1, :], cand[1:2, :]], axis=1)
    own_row = jnp.broadcast_to(row, (N_DEV, N_DEV))
    own_col = own_row.T
    sub = lax.broadcasted_iota(jnp.int32, (N_DEV, N_DEV), 0)
    lane = lax.broadcasted_iota(jnp.int32, (N_DEV, N_DEV), 1)
    asked = (own_col >> 9) == lane
    code = sub * 512 + (own_col & 511)
    first = jnp.min(jnp.where(asked, code, 1 << 20), axis=0, keepdims=True)
    last = jnp.max(jnp.where(asked, code, 0), axis=0, keepdims=True)
    packed = (first & 511) | ((last & 511) << 9)
    codes[me] = packed
    earlier = ((own_col >> 9) == (own_row >> 9)) & (sub < lane)
    rank = jnp.max(earlier.astype(jnp.int32), axis=0, keepdims=True)
    here = (own_row >> 9) == sub

    for (start, rows, order), g in zip(PARTS, bufs):
        g[place(order, me)] = q_ref[start // 32, start % 32 : start % 32 + rows, :]

    pl.semaphore_wait(barrier, len(near))

    def remote(src, dst, s, r, d):
        return pltpu.make_async_remote_copy(
            src_ref=src, dst_ref=dst, send_sem=s, recv_sem=r, device_id=(d,), device_id_type=MESH
        )

    sent = []

    def go(src, dst, s, r, d):
        c = remote(src, dst, s, r, d)
        c.start()
        sent.append(c)

    for i, d in enumerate([shifted(me, "z", k) for k in (1, 2, 3)] + [sibling] + [shifted(sibling, "z", k) for k in (1, 2, 3)]):
        go(codes.at[me], codes.at[me], c_send.at[i], c_recv.at[i], d)
    for p, ((_, rows, order), g) in enumerate(zip(PARTS, bufs)):
        at = place(order, me)
        for k in (1, 2, 3):
            go(g.at[at], g.at[at], q_send.at[p, 0, k - 1], q_recv.at[p, 0, k - 1], shifted(me, order[0], k))

    def arrived(ref, sem):
        pltpu.make_async_copy(ref, ref, sem).wait()

    base8 = (me // 8) * 8
    base32 = (me // 32) * 32
    for i in range(7):
        arrived(codes.at[0], c_recv.at[i])
    for k in (1, 2, 3):
        go(codes.at[pl.ds(base8, 8)], codes.at[pl.ds(base8, 8)], c_send.at[6 + k], c_recv.at[6 + k], shifted(me, "x", k))
    for phase in (1, 2):
        width = 4**phase
        for p, ((_, rows, order), g) in enumerate(zip(PARTS, bufs)):
            at = place(order, me) // width * width
            for k in (1, 2, 3):
                arrived(g.at[pl.ds(0, width // 4)], q_recv.at[p, phase - 1, k - 1])
            block = g.at[pl.ds(at, width)]
            for k in (1, 2, 3):
                go(block, block, q_send.at[p, phase, k - 1], q_recv.at[p, phase, k - 1], shifted(me, order[phase], k))
            if phase == 2:
                go(block, block, sib_send.at[p, 0], sib_recv.at[p, 0], sibling)
        if phase == 1:
            for k in (1, 2, 3):
                arrived(codes.at[pl.ds(0, 8)], c_recv.at[6 + k])
            for k in (1, 2, 3):
                go(codes.at[pl.ds(base32, 32)], codes.at[pl.ds(base32, 32)], c_send.at[9 + k], c_recv.at[9 + k], shifted(me, "y", k))
    for k in (1, 2, 3):
        arrived(codes.at[pl.ds(0, 32)], c_recv.at[9 + k])
    smem_copy = pltpu.make_async_copy(codes, codes_s, smem_sem)
    smem_copy.start()
    for k in (1, 2, 3):
        for p, ((_, rows, order), g) in enumerate(zip(PARTS, bufs)):
            arrived(g.at[pl.ds(0, 16)], q_recv.at[p, 2, k - 1])
            at = place(order, shifted(me, order[2], 4 - k)) // 16 * 16
            block = g.at[pl.ds(at, 16)]
            go(block, block, sib_send.at[p, k], sib_recv.at[p, k], sibling)
    pas_copy.wait()
    smem_copy.wait()
    for p, g in enumerate(bufs):
        for k in range(4):
            arrived(g.at[pl.ds(0, 16)], sib_recv.at[p, k])

    token = lax.broadcasted_iota(jnp.int32, (64, N_DEV), 0)
    half = lax.broadcasted_iota(jnp.int32, (1, N_DEV), 1) < 64

    def pair(j, carry):
        left = []
        lens = []
        right = []
        for r in (2 * j, 2 * j + 1):
            right += [g[place(order, r)] for (_, _, order), g in zip(PARTS, bufs)]
            both = codes_s[r, 0, me]
            for local in (both & 511, both >> 9):
                left.append(pas[local])
                lens.append(len_ref[local])
        sim = lax.dot_general(
            jnp.concatenate(left, axis=0), jnp.concatenate(right, axis=0),
            (((1,), (1,)), ((), ())), preferred_element_type=jnp.float32,
        )
        tops = []
        for i in range(4):
            s = jnp.where(token < lens[i], sim[64 * i : 64 * i + 64, :], -1e30)
            tops.append(jnp.max(s, axis=0, keepdims=True))
        best[0, j] = jnp.where(half, tops[0], tops[2])
        best[1, j] = jnp.where(half, tops[1], tops[3])
        return carry

    lane8 = lax.broadcasted_iota(jnp.int32, (8, N_DEV), 1)

    def group(i, carry):
        lax.fori_loop(8 * i, 8 * i + 8, pair, 0, unroll=True)
        sums = []
        for k in (0, 1):
            v = best[k, pl.ds(8 * i, 8), 0, :]
            for step in (1, 2, 4, 8, 16):
                up = pltpu.roll(v, N_DEV - step, 1)
                down = pltpu.roll(v, step, 1)
                v = v + jnp.where((lane8 // step) % 2 == 0, up, down)
            sums.append(v)
        low = lane8 < 64
        send[0, pl.ds(8 * i, 8), 0, :] = jnp.where(low, sums[0], pltpu.roll(sums[1], 64, 1))
        send[1, pl.ds(8 * i, 8), 0, :] = jnp.where(low, pltpu.roll(sums[0], 64, 1), sums[1])
        for t in range(16):
            r = 16 * i + t

            @pl.when(r != me)
            def _():
                remote(send.at[t % 2, 8 * i + t // 2], recv.at[me], r_send, r_recv, r).start()

            @pl.when(r == me)
            def _():
                recv[me] = send[t % 2, 8 * i + t // 2]

        return carry

    lax.fori_loop(0, 8, group, 0)
    done = remote(recv.at[pl.ds(0, N_DEV - 1)], recv.at[pl.ds(0, N_DEV - 1)], r_send, r_recv, sibling)
    done.wait_recv()

    got = recv[:, 0, :]
    by32, by64, by96 = (pltpu.roll(got, s, 1) for s in (32, 64, 96))
    k0 = jnp.where(lane < 32, got, jnp.where(lane < 96, by32, by64))
    k1 = jnp.where(lane < 32, by64, jnp.where(lane < 96, by96, got))
    mine = jnp.where(here, jnp.where(rank == 0, k0, k1), 0.0)
    total = jnp.sum(mine, axis=0, keepdims=True)
    out_ref[0:1, :] = total[:, :64]
    out_ref[1:2, :] = total[:, 64:]
    done.wait_send()
    for c in sent:
        c.wait_send()


def on_device(queries, passages, lengths, candidates):
    vmem = pl.BlockSpec(memory_space=pltpu.VMEM)
    dma = pltpu.SemaphoreType.DMA
    return pl.pallas_call(
        kernel,
        out_shape=jax.ShapeDtypeStruct((2, 64), jnp.float32),
        in_specs=[vmem, pl.BlockSpec(memory_space=pl.ANY), pl.BlockSpec(memory_space=pltpu.SMEM), vmem],
        out_specs=vmem,
        scratch_shapes=[
            *[pltpu.VMEM((N_DEV, rows, 128), jnp.bfloat16) for _, rows, _ in PARTS],
            pltpu.VMEM((N_DEV, 1, N_DEV), jnp.int32),
            pltpu.VMEM((512, 64, 128), jnp.bfloat16),
            pltpu.SMEM((N_DEV, 1, N_DEV), jnp.int32),
            pltpu.VMEM((2, 64, 1, N_DEV), jnp.float32),
            pltpu.VMEM((2, 64, 1, N_DEV), jnp.float32),
            pltpu.VMEM((N_DEV, 1, N_DEV), jnp.float32),
            dma((3, 3, 3)), dma((3, 3, 3)),
            dma((3, 4)), dma((3, 4)),
            dma((13,)), dma((13,)),
            dma, dma, dma, dma,
        ],
        compiler_params=pltpu.CompilerParams(
            collective_id=0, has_side_effects=True, vmem_limit_bytes=48 * 1024 * 1024
        ),
    )(queries, passages, lengths, candidates)


def solution(mesh):
    return jax.shard_map(
        on_device,
        mesh=mesh,
        in_specs=(P("dev", None, None), P("dev", None, None), P("dev"), P("dev", None)),
        out_specs=P("dev", None),
        check_vma=False,
    )
```

time: 109 us -> 48.1 us (0.44)
  waiting for transfers between devices: 53.9 us -> 0 us
  Pallas kernels: 0 us -> 44.7 us
  blocking collectives: 20.7 us -> 0 us
  local copies, waits for them, and re-layouts: 17.2 us -> 2.64 us
  starting transfers between devices: 11.8 us -> 0 us
  other arithmetic: 2.27 us -> 0 us
  matrix products: 2.16 us -> 0 us
    all_to_all x2 -> x0, waiting for transfers between devices: 53.9 us -> none  [the longest x1 50.8 us: on_device(): lax.all_to_all(block_groups, 'dev', split_axis=0, concat_axis=0, tiled=True)]
    pallas_call x0 -> x1, Pallas kernels: none -> 44.7 us  [on_device(): pl.pallas_call(kernel, out_shape=jax.ShapeDtypeStruct((2, 64), jnp.float3...]
    all_to_all x1 -> x0, blocking collectives: 20.7 us -> none  [on_device(): lax.all_to_all(request_ids, 'dev', split_axis=0, concat_axis=0, tiled=True)]
    gather x4 -> x0, local copies, waits for them, and re-layouts: 12.7 us -> none  [the longest x1 6.4 us: on_device(): block_groups = passages[wanted.reshape(-1)].reshape(count, cap, ptok, dim)]
    all_to_all x2 -> x0, starting transfers between devices: 11.8 us -> none  [the longest x1 7.23 us: on_device(): lax.all_to_all(block_groups, 'dev', split_axis=0, concat_axis=0, tiled=True)]
    unnamed x4 -> x7, local copies, waits for them, and re-layouts: 0.01 us -> 2.64 us
    dot_general x1 -> x0, matrix products: 2.16 us -> none  [on_device(): jnp.einsum('wyf,wrjf->wryj', queries, owned_passages, preferred_element_t...]
    reshape x3 -> x0, local copies, waits for them, and re-layouts: 1.69 us -> none  [the longest x2 1.54 us: on_device(): flat = candidates.reshape(-1)]
  transfers between devices with their start and end apart: 2 -> 0, of which waited for: 2 -> 0; matrix products, arithmetic and copies ran while one was open for 8% -> 0% of each run, Pallas kernels for 0% -> 0%
where the time goes in v1:
time: 48.1 us; the launch traced here: 47.4 us
  Pallas kernels  44.7 us (93%)
  local copies, waits for them, and re-layouts  2.64 us (5%)
    pallas_call x1, Pallas kernels, on_device(): pl.pallas_call(kernel, out_shape=jax.ShapeDtypeStruct((2, 64), jnp.float3...  44.7 us
    unnamed x7, local copies, waits for them, and re-layouts  2.64 us

profile of v1, /device:TPU:1, one launch (start us, length us, event | category | flops | bytes accessed | tf_op | source)
XLA Modules:
  0.0 47.4 jit_solution(16325985749478572732)
XLA Ops:
  0.0 0.0 copy-start
  0.0 0.7 %copy-done = bf16[2,32,128]{2,1,0:T(8,128)(2,1)S(1)} copy-done((bf16[2,32,128]{2,1,0:T(8,128)(2,1)S(1)}, bf16[2,32,128]{2,1,0:T(8,128)(2,1)}, u32[]{:S(2)}) %copy-start) | copy-done | bytes 16408
  0.7 0.0 copy-start.1
  0.7 0.7 %copy-done.1 = s32[512]{0:T(512)S(1)} copy-done((s32[512]{0:T(512)S(1)}, s32[512]{0:T(512)}, u32[]{:S(2)}) %copy-start.1) | copy-done | bytes 2072
  1.4 0.0 copy-start.2
  1.4 0.7 %copy-done.2 = s32[2,64]{1,0:T(2,128)S(1)} copy-done((s32[2,64]{1,0:T(2,128)S(1)}, s32[2,64]{1,0:T(2,128)}, u32[]{:S(2)}) %copy-start.2) | copy-done | bytes 536
  2.1 44.7 %shard_map.46 = f32[2,64]{1,0:T(2,128)S(1)} custom-call(bf16[2,32,128]{2,1,0:T(8,128)(2,1)S(1)} %copy-done, bf16[512,64,128]{2,1,0:T(8,128)(2,1)} %pas_hbm.1, s32[512]{0:T(512)S(1)} %copy-done.1, s32[2,64]{1,0:T(2,128)S(1)} %copy-done.2), custom_call_target="tpu_custom_call" | custom-call | tf_op jit(solution)/shard_map/pallas_call | solution.py:206
  46.8 0.6 %copy.6 = f32[2,64]{1,0:T(2,128)} copy(f32[2,64]{1,0:T(2,128)S(1)} %shard_map.46) | data formatting | bytes 1024
Async XLA Ops:
  0.0 0.7 %copy-start = (bf16[2,32,128]{2,1,0:T(8,128)(2,1)S(1)}, bf16[2,32,128]{2,1,0:T(8,128)(2,1)}, u32[]{:S(2)}) copy-start(bf16[2,32,128]{2,1,0:T(8,128)(2,1)} %q_ref.1) | copy-start | bytes 49156
  0.7 0.7 %copy-start.1 = (s32[512]{0:T(512)S(1)}, s32[512]{0:T(512)}, u32[]{:S(2)}) copy-start(s32[512]{0:T(512)} %len_ref.1) | copy-start | bytes 6148
  1.4 0.7 %copy-start.2 = (s32[2,64]{1,0:T(2,128)S(1)}, s32[2,64]{1,0:T(2,128)}, u32[]{:S(2)}) copy-start(s32[2,64]{1,0:T(2,128)} %cand_ref.1) | copy-start | bytes 1540
